TPU v7x, 32 devices: a whole 2x2x4 slice. The times are simulated.
32 devices in a mesh: segment: 2 (over core), space: 16 (over z, y, x).
Axes of the slice: x: 2, y: 2, z: 4, core: 2. Of those that a mesh axis runs over, the one named last changes fastest.
Arguments:
- stash_down: bfloat16 [2, 64, 32, 384], P('segment', 'space'), may hold values from -6 to 6
- stash_up: bfloat16 [2, 64, 32, 384], P('segment', 'space'), may hold values from -6 to 6
- grad_down: bfloat16 [64, 32, 384], P('space'), may hold values from -6 to 6
- grad_up: bfloat16 [64, 32, 384], P('space'), may hold values from -6 to 6
- dw_kernel: bfloat16 [2, 2, 49, 384], P('segment'), as said below
- norm_gain: float32 [2, 2, 384], P('segment'), as said below
- norm_bias: float32 [2, 2, 384], P('segment'), as said below
- w_in: bfloat16 [2, 2, 384, 1536], P('segment', None, 'space'), as said below
- b_in: float32 [2, 2, 1536], P('segment'), as said below
- w_out: bfloat16 [2, 2, 1536, 384], P('segment', None, 'space'), as said below
- layer_scale: float32 [2, 2, 384], P('segment'), as said below
Outputs:
- input_grad_down: bfloat16 [2, 64, 32, 384], P('segment', 'space')
- input_grad_up: bfloat16 [2, 64, 32, 384], P('segment', 'space')
- w_out_grad: float32 [2, 1536, 384], P('segment', 'space')
- kernel_grad: float32 [2, 49, 384], P('segment')
Inputs may be any that keep to these rules, and one draw needn't show every extreme that they name: `dw_kernel`: entry [s, 1] equals entry [1 - s, 0] for every s. `norm_gain`: entry [s, 1] equals entry [1 - s, 0] for every s. `norm_bias`: entry [s, 1] equals entry [1 - s, 0] for every s. `w_in`: entry [s, 1] equals entry [1 - s, 0] for every s. `b_in`: entry [s, 1] equals entry [1 - s, 0] for every s. `w_out`: entry [s, 1] equals entry [1 - s, 0] for every s. `layer_scale`: entry [s, 1] equals entry [1 - s, 0] for every s.
All inputs are finite; a program needn't handle non-finite values.
Results may differ from a plain program's by a relative error of at most 0.0075.
Values may be sent and summed in bfloat16 or wider, within the bound.
A program may use at most 64 MiB of HBM per device.

v0:
```python
import math
import jax
import jax.numpy as jnp
from jax import lax
from jax.sharding import PartitionSpec as P

KSIDE = 7


def padded_2(cells, sides, width):
    for axis, dim in sides:
        count = lax.axis_size(axis)
        ends = count - 1
        head = lax.slice_in_dim(cells, 0, width, axis=dim)
        tail = lax.slice_in_dim(cells, cells.shape[dim] - width, cells.shape[dim], axis=dim)
        cells = jnp.concatenate(
            [
                lax.ppermute(tail, axis, [(i, (i + 1) % count) for i in range(ends)]),
                cells,
                lax.ppermute(head, axis, [((i + 1) % count, i) for i in range(ends)]),
            ],
            axis=dim,
        )
    return cells


def passed_along(shard, axis, by):
    devices = lax.axis_size(axis)
    pairs = [(i, i + by) for i in range(devices) if 0 <= i + by < devices]
    return lax.ppermute(shard, axis, pairs)


def as_sent(shard):
    return jax.tree.map(lambda a: a.astype(jnp.bfloat16) if a.dtype == jnp.float32 else a, shard)


def swapped(block, axis, stride):
    count = lax.axis_size(axis)
    route = []
    for low in range(count):
        high = low | 1 << stride
        if high != low and high < count:
            route += [(low, high), (high, low)]
    return lax.ppermute(block, axis, route)


def gelu_parts(a):
    inner = 0.7978845608 * (a + 0.044715 * a * a * a)
    th = jnp.tanh(inner)
    value = 0.5 * a * (1.0 + th)
    slope = 0.5 * (1.0 + th) + 0.5 * a * (1.0 - th * th) * 0.7978845608 * (1.0 + 0.134145 * a * a)
    return (value, slope)


def grouped_conv(padded, filters):
    chans = padded.shape[2]
    result = lax.conv_general_dilated(
        padded[None],
        filters,
        (1, 1),
        "VALID",
        dimension_numbers=("NHWC", "HWIO", "NHWC"),
        feature_group_count=chans,
        precision=lax.Precision.HIGHEST,
    )
    return result[0]


def depthwise(padded, kernel):
    chans = kernel.shape[1]
    filters = kernel.reshape(KSIDE, KSIDE, 1, chans)
    return grouped_conv(padded, filters)


def depthwise_back(padded, kernel):
    chans = kernel.shape[1]
    filters = kernel.reshape(KSIDE, KSIDE, 1, chans)[::-1, ::-1]
    return grouped_conv(padded, filters)


def kernel_terms(padded, grad):
    rows, cols, chans = grad.shape
    filters = grad.reshape(rows, cols, 1, chans)
    return grouped_conv(padded, filters).reshape(KSIDE * KSIDE, chans)


def pointwise_back(v, g, gain, bias, w_first, b_first, w_second, scale_res):
    rows, cols, chans = v.shape
    flat = v.reshape(rows * cols, chans)
    mean_v = jnp.mean(flat, axis=1, keepdims=True)
    centred = flat - mean_v
    rs = lax.rsqrt(jnp.mean(centred * centred, axis=1, keepdims=True) + 1e-06)
    nh = centred * rs
    normed = (nh * gain + bias).astype(jnp.bfloat16)
    pre = jnp.dot(normed, w_first, preferred_element_type=jnp.float32) + b_first
    value, slope = gelu_parts(pre)
    hidden = value.astype(jnp.bfloat16)
    outer = (g.reshape(rows * cols, chans).astype(jnp.float32) * scale_res).astype(jnp.bfloat16)
    dh = lax.dot_general(
        outer, w_second, (((1,), (1,)), ((), ())), preferred_element_type=jnp.float32
    )
    da = (dh * slope).astype(jnp.bfloat16)
    dn = lax.dot_general(da, w_first, (((1,), (1,)), ((), ())), preferred_element_type=jnp.float32)
    q = dn * gain
    du = rs * (
        q - jnp.mean(q, axis=1, keepdims=True) - nh * jnp.mean(q * nh, axis=1, keepdims=True)
    )
    return (du.astype(jnp.bfloat16).reshape(rows, cols, chans), hidden, outer)


def per_device(
    stash_down,
    stash_up,
    grad_down,
    grad_up,
    dw_kernel,
    norm_gain,
    norm_bias,
    w_in,
    b_in,
    w_out,
    layer_scale,
):
    segments = lax.axis_size("segment")
    me = lax.axis_index("segment")
    half = KSIDE // 2
    rows, cols, chans = (stash_down.shape[1], stash_down.shape[2], stash_down.shape[3])
    hidden_units = w_in.shape[3]
    norm = 1.0 / math.sqrt(2.0 * rows * lax.axis_size("space") * cols)
    w_in_all, w_out_all = (
        lax.all_gather(w_in, "space", axis=2, tiled=True),
        lax.all_gather(w_out, "space", axis=2, tiled=True),
    )
    x_down = stash_down[0]
    x_up = stash_up[0]
    rimmed_both = padded_2(jnp.stack([x_down, x_up]), (("space", 1),), half)
    down_in = grad_down
    up_in = grad_up
    out_down = jnp.zeros_like(grad_down)
    out_up = jnp.zeros_like(grad_up)
    tokens = rows * cols
    hid_down = jnp.zeros((tokens, hidden_units), jnp.bfloat16)
    hid_up = jnp.zeros((tokens, hidden_units), jnp.bfloat16)
    outer_down = jnp.zeros((tokens, chans), jnp.bfloat16)
    outer_up = jnp.zeros((tokens, chans), jnp.bfloat16)
    kern_down = jnp.zeros((KSIDE * KSIDE, chans), jnp.float32)
    kern_up = jnp.zeros((KSIDE * KSIDE, chans), jnp.float32)
    for step in range(segments):
        on_up = me == step
        on_down = me == segments - 1 - step
        active = jnp.logical_or(on_up, on_down)
        pick = on_up.astype(jnp.int32)

        def select(array):
            return lax.dynamic_index_in_dim(array[0], pick, 0, keepdims=False)

        rimmed = jnp.where(on_up, rimmed_both[1], rimmed_both[0])
        padded = jnp.pad(rimmed.astype(jnp.float32), ((0, 0), (half, half), (0, 0)))
        g = jnp.where(on_up, up_in, down_in)
        kern = select(dw_kernel).astype(jnp.float32)

        def front_live():
            v = depthwise(padded, kern)
            return pointwise_back(
                v,
                g,
                select(norm_gain),
                select(norm_bias),
                select(w_in_all),
                select(b_in),
                select(w_out_all),
                select(layer_scale),
            )

        def front_spare():
            return (
                jnp.zeros((rows, cols, chans), jnp.bfloat16),
                jnp.zeros((tokens, hidden_units), jnp.bfloat16),
                jnp.zeros((tokens, chans), jnp.bfloat16),
            )

        du, hidden, outer = lax.cond(active, front_live, front_spare)
        du_rimmed = padded_2(du, (("space", 0),), half)

        def back_live():
            du_pad = jnp.pad(du_rimmed.astype(jnp.float32), ((0, 0), (half, half), (0, 0)))
            dx_new = (g.astype(jnp.float32) + depthwise_back(du_pad, kern)).astype(jnp.bfloat16)
            dk_new = kernel_terms(padded, du.astype(jnp.float32))
            return (dx_new, dk_new)

        def back_spare():
            return (
                jnp.zeros((rows, cols, chans), jnp.bfloat16),
                jnp.zeros((KSIDE * KSIDE, chans), jnp.float32),
            )

        dx, dk = lax.cond(active, back_live, back_spare)
        out_down = jnp.where(on_down, dx, out_down)
        out_up = jnp.where(on_up, dx, out_up)
        kern_down = jnp.where(on_down, dk, kern_down)
        kern_up = jnp.where(on_up, dk, kern_up)
        hid_down = jnp.where(on_down, hidden, hid_down)
        hid_up = jnp.where(on_up, hidden, hid_up)
        outer_down = jnp.where(on_down, outer, outer_down)
        outer_up = jnp.where(on_up, outer, outer_up)
        if step + 1 < segments:
            down_in = passed_along(dx, "segment", -1)
            up_in = passed_along(dx, "segment", 1)
    levels = segments.bit_length() - 1
    for bit in range(levels):
        kern_up = swapped(as_sent(kern_up), "segment", bit).astype(kern_up.dtype)
    share = w_out.shape[2]
    joined = jnp.concatenate([hid_up, outer_up], axis=1)
    for bit in range(levels):
        joined = swapped(joined, "segment", bit)
    all_hidden = jnp.concatenate([hid_down, joined[:, :hidden_units]], axis=0)
    all_outer = jnp.concatenate([outer_down, joined[:, hidden_units:]], axis=0)
    columns = lax.slice_in_dim(all_hidden, 0, share * lax.axis_size("space"), axis=1)
    w_grad = lax.psum_scatter(
        lax.dot_general(
            columns, all_outer, (((0,), (0,)), ((), ())), preferred_element_type=jnp.float32
        )
        * norm,
        "space",
        scatter_dimension=0,
        tiled=True,
    )
    k_grad = lax.psum(kern_down + kern_up, "space") * norm
    return (out_down[None], out_up[None], w_grad[None], k_grad[None])


def solution(mesh):
    return jax.shard_map(
        per_device,
        mesh=mesh,
        in_specs=(
            P("segment", "space", None, None),
            P("segment", "space", None, None),
            P("space", None, None),
            P("space", None, None),
            P("segment", None, None, None),
            P("segment", None, None),
            P("segment", None, None),
            P("segment", None, "space", None),
            P("segment", None, None),
            P("segment", None, "space", None),
            P("segment", None, None),
        ),
        out_specs=(
            P("segment", "space", None, None),
            P("segment", "space", None, None),
            P("segment", "space", None),
            P("segment", None, None),
        ),
        check_vma=False,
    )
```

profile of v0, /device:TPU:0, one launch (start us, length us, event | category | flops | bytes accessed | tf_op | source)
XLA Modules:
  0.0 438.8 jit_solution(5692250722293077002)
XLA Ops:
  11.9 5.5 %collective-permute-start = (bf16[2,3,32,384]{3,2,1,0:T(8,128)(2,1)S(1)}, bf16[2,3,32,384]{3,2,1,0:T(8,128)(2,1)S(1)}, u32[]{:S(2)}, u32[]{:S(2)}) collective-permute-start(bf16[2,3,32,384]{3,2,1,0:T(8,128)(2,1)S(1)} %get-tuple-element.140), channel_id=1, source_target_pairs={{0,1},{1,2},{2,3},{3,4},{4,5},{5,6},{6,7},{7,8},{8,9},{9,10},{10,1... | collective-permute-start | bytes 442376 | tf_op jit(solution)/shard_map/ppermute | solution.py:18
  19.5 5.1 %collective-permute-done = bf16[2,3,32,384]{3,2,1,0:T(8,128)(2,1)S(1)} collective-permute-done((bf16[2,3,32,384]{3,2,1,0:T(8,128)(2,1)S(1)}, bf16[2,3,32,384]{3,2,1,0:T(8,128)(2,1)S(1)}, u32[]{:S(2)}, u32[]{:S(2)}) %collective-permute-start) | collective-permute-done | bytes 147488 | tf_op jit(solution)/shard_map/ppermute | solution.py:18
  24.8 51.0 %all-gather.3.cloned.1.call-done = bf16[1,2,1536,384]{3,2,1,0:T(8,128)(2,1)} async-done(((bf16[1,2,96,384]{3,2,1,0:T(8,128)(2,1)}), bf16[1,2,1536,384]{3,2,1,0:T(8,128)(2,1)}) %all-gather.3.cloned.1.call-update) | async-done | bytes 2359312 | tf_op jit(solution)/shard_map/all_gather | solution.py:132
  75.8 63.9 %all-gather.5.cloned.1.call-done = bf16[1,2,384,1536]{3,2,1,0:T(8,128)(2,1)} async-done(((bf16[1,2,24,1536]{3,2,1,0:T(8,128)(2,1)}), bf16[1,2,384,1536]{3,2,1,0:T(8,128)(2,1)}) %all-gather.5.cloned.1.call-update) | async-done | bytes 2359312 | tf_op jit(solution)/shard_map/all_gather | solution.py:131
  139.7 10.4 %conditional.4 = (bf16[4,32,384]{2,1,0:T(8,128)(2,1)S(1)}, bf16[128,1536]{1,0:T(8,128)(2,1)S(1)}, bf16[128,384]{1,0:T(8,128)(2,1)S(1)}) conditional(s32[]{:T(128)} %convert_element_type.123, () %tuple.42, (f32[10,38,384]{2,1,0:T(8,128)S(1)}, f32[49,384]{1,0:T(8,128)S(1)}, bf16[4,32,384]{2,1,0:T(8,128)(2,1)S(1)}, s32[]{:T(128)}, ...), branch_computations={%region_0.1_spmd, %region_1.6_spmd} | conditional | flops 488964224 | bytes 9116234 | solution.py:182
  139.8 4.1 fusion.113
  145.5 1.8 multiply_convert_fusion
  147.3 2.6 fusion.111
  151.4 4.5 %collective-permute-start.2 = (bf16[3,32,384]{2,1,0:T(8,128)(2,1)S(1)}, bf16[3,32,384]{2,1,0:T(8,128)(2,1)S(1)}, u32[]{:S(2)}, u32[]{:S(2)}) collective-permute-start(bf16[3,32,384]{2,1,0:T(8,128)(2,1)S(1)} %get-tuple-element.144), channel_id=1, source_target_pairs={{0,1},{1,2},{2,3},{3,4},{4,5},{5,6},{6,7},{7,8},{8,9},{9,10},{10,1... | collective-permute-start | bytes 221192 | tf_op jit(solution)/shard_map/ppermute | solution.py:18
  158.0 4.3 conditional.5
  158.2 1.8 fusion.47
  160.0 2.3 convolution_reduce_fusion
  164.9 1.8 collective-permute-done.5
  166.8 10.4 %conditional.6 = (bf16[4,32,384]{2,1,0:T(8,128)(2,1)S(1)}, bf16[128,1536]{1,0:T(8,128)(2,1)S(1)}, bf16[128,384]{1,0:T(8,128)(2,1)S(1)}) conditional(s32[]{:T(128)} %convert_element_type.123, () %tuple.45, (f32[10,38,384]{2,1,0:T(8,128)S(1)}, f32[49,384]{1,0:T(8,128)S(1)}, bf16[4,32,384]{2,1,0:T(8,128)(2,1)S(1)}, s32[]{:T(128)}, ...), branch_computations={%region_8.9_spmd, %region_9.14_spmd} | conditional | flops 488964224 | bytes 9116234 | solution.py:182
  166.9 4.1 fusion.116
  174.4 2.6 fusion.112
  178.5 4.9 %collective-permute-start.6 = (bf16[3,32,384]{2,1,0:T(8,128)(2,1)S(1)}, bf16[3,32,384]{2,1,0:T(8,128)(2,1)S(1)}, u32[]{:S(2)}, u32[]{:S(2)}) collective-permute-start(bf16[3,32,384]{2,1,0:T(8,128)(2,1)S(1)} %get-tuple-element.142), channel_id=1, source_target_pairs={{0,1},{1,2},{2,3},{3,4},{4,5},{5,6},{6,7},{7,8},{8,9},{9,10},{10,1... | collective-permute-start | bytes 221192 | tf_op jit(solution)/shard_map/ppermute | solution.py:18
  184.1 2.8 collective-permute-done.6
  186.9 4.3 conditional.7
  187.1 1.8 fusion.98
  188.9 2.2 convolution_reduce_fusion.1
  193.2 2.0 convolution_multiply_fusion.2
  196.0 103.2 %all-reduce.6.cloned.1.call-done = f32[49,384]{1,0:T(8,128)} async-done(((f32[49,384]{1,0:T(8,128)}), f32[49,384]{1,0:T(8,128)}) %all-reduce.6.cloned.1.call-update) | async-done | bytes 75280 | tf_op jit(solution)/shard_map/psum | solution.py:228
  300.8 131.5 %reduce-scatter.2.cloned.1.call-done = f32[96,384]{1,0:T(8,128)} async-done(((f32[1536,384]{1,0:T(8,128)}), f32[96,384]{1,0:T(8,128)}) %reduce-scatter.2.cloned.1.call-update) | async-done | bytes 147472 | tf_op jit(solution)/shard_map/reduce_scatter | solution.py:219
  (99 shorter events, 24.9 us)
Async XLA Ops:
  7.2 68.6 %all-gather.3.cloned.1.call-start = ((), (), s32[]{:S(2)}) async-start(), calls=%async_computation.1 | async-start | bytes 2506752 | tf_op jit(solution)/shard_map/all_gather | solution.py:132
  7.9 131.8 %copy-start = (f32[1,2,1536]{2,1,0:T(2,128)S(1)}, f32[1,2,1536]{2,1,0:T(2,128)}, u32[]{:S(2)}) copy-start(f32[1,2,1536]{2,1,0:T(2,128)} %param.27) | copy-start | bytes 36868
  7.9 131.8 %copy-start.1 = (f32[1,2,384]{2,1,0:T(2,128)S(1)}, f32[1,2,384]{2,1,0:T(2,128)}, u32[]{:S(2)}) copy-start(f32[1,2,384]{2,1,0:T(2,128)} %param.29) | copy-start | bytes 9220
  7.9 131.7 %copy-start.2 = (f32[1,2,384]{2,1,0:T(2,128)S(1)}, f32[1,2,384]{2,1,0:T(2,128)}, u32[]{:S(2)}) copy-start(f32[1,2,384]{2,1,0:T(2,128)} %param.24) | copy-start | bytes 9220
  7.9 131.7 %copy-start.3 = (f32[1,2,384]{2,1,0:T(2,128)S(1)}, f32[1,2,384]{2,1,0:T(2,128)}, u32[]{:S(2)}) copy-start(f32[1,2,384]{2,1,0:T(2,128)} %param.25) | copy-start | bytes 9220
  7.9 131.7 %all-gather.5.cloned.1.call-start = ((), (), s32[]{:S(2)}) async-start(), calls=%async_computation.2 | async-start | bytes 2506752 | tf_op jit(solution)/shard_map/all_gather | solution.py:131
  8.7 290.5 %all-reduce.6.cloned.1.call-start = ((), (), s32[]{:S(2)}) async-start(), calls=%async_computation.4 | async-start | bytes 172032 | tf_op jit(solution)/shard_map/psum | solution.py:228
  10.6 8.9 %collective-permute-start.1 = (bf16[2,3,32,384]{3,2,1,0:T(8,128)(2,1)S(1)}, bf16[2,3,32,384]{3,2,1,0:T(8,128)(2,1)S(1)}, u32[]{:S(2)}, u32[]{:S(2)}) collective-permute-start(bf16[2,3,32,384]{3,2,1,0:T(8,128)(2,1)S(1)} %get-tuple-element.141), channel_id=1, source_target_pairs={{1,0},{2,1},{3,2},{4,3},{5,4},{6,5},{7,6},{8,7},{9,8},{10,9},{11,1... | collective-permute-start | bytes 442376 | tf_op jit(solution)/shard_map/ppermute | solution.py:20
  11.9 12.7 %collective-permute-start = (bf16[2,3,32,384]{3,2,1,0:T(8,128)(2,1)S(1)}, bf16[2,3,32,384]{3,2,1,0:T(8,128)(2,1)S(1)}, u32[]{:S(2)}, u32[]{:S(2)}) collective-permute-start(bf16[2,3,32,384]{3,2,1,0:T(8,128)(2,1)S(1)} %get-tuple-element.140), channel_id=1, source_target_pairs={{0,1},{1,2},{2,3},{3,4},{4,5},{5,6},{6,7},{7,8},{8,9},{9,10},{10,1... | collective-permute-start | bytes 442376 | tf_op jit(solution)/shard_map/ppermute | solution.py:18
  150.1 6.2 %collective-permute-start.3 = (bf16[3,32,384]{2,1,0:T(8,128)(2,1)S(1)}, bf16[3,32,384]{2,1,0:T(8,128)(2,1)S(1)}, u32[]{:S(2)}, u32[]{:S(2)}) collective-permute-start(bf16[3,32,384]{2,1,0:T(8,128)(2,1)S(1)} %get-tuple-element.145), channel_id=1, source_target_pairs={{1,0},{2,1},{3,2},{4,3},{5,4},{6,5},{7,6},{8,7},{9,8},{10,9},{11,1... | collective-permute-start | bytes 221192 | tf_op jit(solution)/shard_map/ppermute | solution.py:20
  151.4 6.5 %collective-permute-start.2 = (bf16[3,32,384]{2,1,0:T(8,128)(2,1)S(1)}, bf16[3,32,384]{2,1,0:T(8,128)(2,1)S(1)}, u32[]{:S(2)}, u32[]{:S(2)}) collective-permute-start(bf16[3,32,384]{2,1,0:T(8,128)(2,1)S(1)} %get-tuple-element.144), channel_id=1, source_target_pairs={{0,1},{1,2},{2,3},{3,4},{4,5},{5,6},{6,7},{7,8},{8,9},{9,10},{10,1... | collective-permute-start | bytes 221192 | tf_op jit(solution)/shard_map/ppermute | solution.py:18
  162.3 2.7 collective-permute-start.4
  163.6 3.2 collective-permute-start.5
  177.2 6.9 %collective-permute-start.7 = (bf16[3,32,384]{2,1,0:T(8,128)(2,1)S(1)}, bf16[3,32,384]{2,1,0:T(8,128)(2,1)S(1)}, u32[]{:S(2)}, u32[]{:S(2)}) collective-permute-start(bf16[3,32,384]{2,1,0:T(8,128)(2,1)S(1)} %get-tuple-element.143), channel_id=1, source_target_pairs={{1,0},{2,1},{3,2},{4,3},{5,4},{6,5},{7,6},{8,7},{9,8},{10,9},{11,1... | collective-permute-start | bytes 221192 | tf_op jit(solution)/shard_map/ppermute | solution.py:20
  178.5 8.3 %collective-permute-start.6 = (bf16[3,32,384]{2,1,0:T(8,128)(2,1)S(1)}, bf16[3,32,384]{2,1,0:T(8,128)(2,1)S(1)}, u32[]{:S(2)}, u32[]{:S(2)}) collective-permute-start(bf16[3,32,384]{2,1,0:T(8,128)(2,1)S(1)} %get-tuple-element.142), channel_id=1, source_target_pairs={{0,1},{1,2},{2,3},{3,4},{4,5},{5,6},{6,7},{7,8},{8,9},{9,10},{10,1... | collective-permute-start | bytes 221192 | tf_op jit(solution)/shard_map/ppermute | solution.py:18
  183.6 9.6 %collective-permute-start.8 = (bf16[128,1920]{1,0:T(8,128)(2,1)S(1)}, bf16[128,1920]{1,0:T(8,128)(2,1)S(1)}, u32[]{:S(2)}, u32[]{:S(2)}) collective-permute-start(bf16[128,1920]{1,0:T(8,128)(2,1)S(1)} %pad_maximum_fusion.1), channel_id=1, source_target_pairs={{0,16},{16,0},{1,17},{17,1},{2,18},{18,2},{3,19},{19,3},{4,20},{20... | collective-permute-start | bytes 1474568 | tf_op jit(solution)/shard_map/ppermute | solution.py:44
  191.2 1.3 collective-permute-start.9
  193.1 239.2 %reduce-scatter.2.cloned.1.call-start = ((), (), s32[]{:S(2)}) async-start(), calls=%async_computation.3 | async-start | bytes 2506752 | tf_op jit(solution)/shard_map/reduce_scatter | solution.py:219
Sparse Core Ops, SparseCore 0:
  10.7 65.0 all-gather.2
  78.5 61.1 all-gather.4
  193.2 105.9 all-reduce.5
  304.5 127.6 reduce-scatter.1
where the time goes:
time: 439 us
  waiting for transfers between devices  364 us (83%)
  matrix products  27 us (6%)
  starting transfers between devices  21.7 us (5%)
  between operations  14.1 us (3%)
  other arithmetic  6.63 us (2%)
  local copies, waits for them, and re-layouts  4.77 us (1%)
    reduce_scatter x1, waiting for transfers between devices, per_device(): lax.psum_scatter(lax.dot_general(columns, all_outer, (((0,), (0,)), ((),...  131 us
    psum x1, waiting for transfers between devices, per_device(): k_grad = lax.psum(kern_down + kern_up, 'space') * norm  103 us
    all_gather x1, waiting for transfers between devices, per_device(): lax.all_gather(w_in, 'space', axis=2, tiled=True)  63.9 us
    all_gather x1, waiting for transfers between devices, per_device(): lax.all_gather(w_out, 'space', axis=2, tiled=True)  51 us
    conv_general_dilated x6, matrix products, grouped_conv(): lax.conv_general_dilated(padded[None], filters, (1, 1), 'VALID', dimensio...  16.2 us
    ppermute x3, starting transfers between devices, padded_2(): lax.ppermute(tail, axis, [(i, (i + 1) % count) for i in range(ends)])  14.9 us
    ppermute x3, waiting for transfers between devices, padded_2(): lax.ppermute(tail, axis, [(i, (i + 1) % count) for i in range(ends)])  9.47 us
  transfers between devices with their start and end apart: 14, of which 11 were waited for; matrix products, arithmetic and copies ran while one was open for 3% of the time, Pallas kernels for 0%

commit v1 on v0

--- a/solution.py
+++ b/solution.py
@@ -5,6 +5,22 @@
 from jax.sharding import PartitionSpec as P
 
 KSIDE = 7
+
+
+def collect(x, axis, dim):
+    ways, here, step = (lax.axis_size(axis), lax.axis_index(axis), x.shape[dim])
+    shape = [n * ways if d == dim else n for d, n in enumerate(x.shape)]
+    full = lax.dynamic_update_slice_in_dim(jnp.zeros(shape, x.dtype), x, here * step, axis=dim)
+    going_up = going_down = x
+    for far in range(1, ways // 2 + 1):
+        going_up = lax.ppermute(going_up, axis, [(d, (d + 1) % ways) for d in range(ways)])
+        full = lax.dynamic_update_slice_in_dim(full, going_up, (here - far) % ways * step, axis=dim)
+        if 2 * far < ways:
+            going_down = lax.ppermute(going_down, axis, [(d, (d - 1) % ways) for d in range(ways)])
+            full = lax.dynamic_update_slice_in_dim(
+                full, going_down, (here + far) % ways * step, axis=dim
+            )
+    return full
 
 
 def padded_2(cells, sides, width):
@@ -128,7 +144,7 @@
     hidden_units = w_in.shape[3]
     norm = 1.0 / math.sqrt(2.0 * rows * lax.axis_size("space") * cols)
     w_in_all, w_out_all = (
-        lax.all_gather(w_in, "space", axis=2, tiled=True),
+        collect(w_in, "space", 2),
         lax.all_gather(w_out, "space", axis=2, tiled=True),
     )
     x_down = stash_down[0]

time: 439 us -> 400 us (0.911)
  waiting for transfers between devices: 364 us -> 277 us
  starting transfers between devices: 21.7 us -> 59.2 us
  other arithmetic: 6.63 us -> 13.2 us
    all_gather x1 -> x0, waiting for transfers between devices: 63.9 us -> none  [per_device(): lax.all_gather(w_in, 'space', axis=2, tiled=True)]
    all_gather x1, waiting for transfers between devices: 51 us -> 2.59 us  [per_device(): lax.all_gather(w_out, 'space', axis=2, tiled=True)]
    ppermute x0 -> x15, starting transfers between devices: none -> 42.8 us  [the longest x7 33.3 us: collect(): lax.ppermute(going_down, axis, [(d, (d - 1) % ways) for d in range(ways)])]
    ppermute x0 -> x15, waiting for transfers between devices: none -> 32.4 us  [the longest x8 29.2 us: collect(): lax.ppermute(going_up, axis, [(d, (d + 1) % ways) for d in range(ways)])]
    ppermute x3, waiting for transfers between devices: 9.47 us -> 0.01 us  [padded_2(): lax.ppermute(tail, axis, [(i, (i + 1) % count) for i in range(ends)])]
    ppermute x3, waiting for transfers between devices: 0.79 us -> 7.88 us  [padded_2(): lax.ppermute(head, axis, [((i + 1) % count, i) for i in range(ends)])]
    ppermute x3, starting transfers between devices: 14.9 us -> 9.69 us  [padded_2(): lax.ppermute(tail, axis, [(i, (i + 1) % count) for i in range(ends)])]
  transfers between devices with their start and end apart: 14 -> 28, of which waited for: 11 -> 17; matrix products, arithmetic and copies ran while one was open for 3% -> 5% of each run, Pallas kernels for 0% -> 0%
where the time goes in v1:
time: 400 us; the launch traced here: 399 us
  waiting for transfers between devices  277 us (69%)
  starting transfers between devices  59.2 us (15%)
  matrix products  26.6 us (7%)
  between operations  14.3 us (4%)
  other arithmetic  13.2 us (3%)
  local copies, waits for them, and re-layouts  8.8 us (2%)
    reduce_scatter x1, waiting for transfers between devices, per_device(): lax.psum_scatter(lax.dot_general(columns, all_outer, (((0,), (0,)), ((),...  131 us
    psum x1, waiting for transfers between devices, per_device(): k_grad = lax.psum(kern_down + kern_up, 'space') * norm  100 us
    ppermute x7, starting transfers between devices, collect(): lax.ppermute(going_down, axis, [(d, (d - 1) % ways) for d in range(ways)])  33.3 us
    ppermute x8, waiting for transfers between devices, collect(): lax.ppermute(going_up, axis, [(d, (d + 1) % ways) for d in range(ways)])  29.2 us
    conv_general_dilated x6, matrix products, grouped_conv(): lax.conv_general_dilated(padded[None], filters, (1, 1), 'VALID', dimensio...  15.6 us
    ppermute x3, starting transfers between devices, padded_2(): lax.ppermute(tail, axis, [(i, (i + 1) % count) for i in range(ends)])  9.69 us
    ppermute x8, starting transfers between devices, collect(): lax.ppermute(going_up, axis, [(d, (d + 1) % ways) for d in range(ways)])  9.42 us
  transfers between devices with their start and end apart: 28, of which 17 were waited for; matrix products, arithmetic and copies ran while one was open for 5% of the time, Pallas kernels for 0%

profile of v1, /device:TPU:0, one launch (start us, length us, event | category | flops | bytes accessed | tf_op | source)
XLA Modules:
  0.0 399.3 jit_solution(13067269239079098653)
XLA Ops:
  10.2 4.1 %collective-permute-start.3 = (bf16[1,2,24,1536]{3,2,1,0:T(8,128)(2,1)}, bf16[1,2,24,1536]{3,2,1,0:T(8,128)(2,1)S(1)}, u32[]{:S(2)}, u32[]{:S(2)}) collective-permute-start(bf16[1,2,24,1536]{3,2,1,0:T(8,128)(2,1)} %param.26), channel_id=1, source_target_pairs={{0,15},{1,0},{2,1},{3,2},{4,3},{5,4},{6,5},{7,6},{8,7},{9,8},{10,9... | collective-permute-start | bytes 442376 | tf_op jit(solution)/shard_map/ppermute | solution.py:19
  23.3 3.3 collective-permute-start.5
  29.6 3.9 collective-permute-done.4
  35.8 3.2 collective-permute-start.7
  39.1 3.9 collective-permute-done.6
  44.3 4.3 %collective-permute-start.9 = (bf16[1,2,24,1536]{3,2,1,0:T(8,128)(2,1)S(1)}, bf16[1,2,24,1536]{3,2,1,0:T(8,128)(2,1)S(1)}, u32[]{:S(2)}, u32[]{:S(2)}) collective-permute-start(bf16[1,2,24,1536]{3,2,1,0:T(8,128)(2,1)S(1)} %collective-permute-done.7), channel_id=1, source_target_pairs={{0,15},{1,0},{2,1},{3,2},{4,3},{5,4},{6,5},{7,6},{8,7},{9,8},{10,9... | collective-permute-start | bytes 442376 | tf_op jit(solution)/shard_map/ppermute | solution.py:19
  48.6 3.3 collective-permute-done.8
  52.1 6.2 %collective-permute-start.11 = (bf16[1,2,24,1536]{3,2,1,0:T(8,128)(2,1)S(1)}, bf16[1,2,24,1536]{3,2,1,0:T(8,128)(2,1)S(1)}, u32[]{:S(2)}, u32[]{:S(2)}) collective-permute-start(bf16[1,2,24,1536]{3,2,1,0:T(8,128)(2,1)S(1)} %collective-permute-done.9), channel_id=1, source_target_pairs={{0,15},{1,0},{2,1},{3,2},{4,3},{5,4},{6,5},{7,6},{8,7},{9,8},{10,9... | collective-permute-start | bytes 442376 | tf_op jit(solution)/shard_map/ppermute | solution.py:19
  62.8 6.0 %collective-permute-start.13 = (bf16[1,2,24,1536]{3,2,1,0:T(8,128)(2,1)S(1)}, bf16[1,2,24,1536]{3,2,1,0:T(8,128)(2,1)S(1)}, u32[]{:S(2)}, u32[]{:S(2)}) collective-permute-start(bf16[1,2,24,1536]{3,2,1,0:T(8,128)(2,1)S(1)} %collective-permute-done.11), channel_id=1, source_target_pairs={{0,15},{1,0},{2,1},{3,2},{4,3},{5,4},{6,5},{7,6},{8,7},{9,8},{10,9... | collective-permute-start | bytes 442376 | tf_op jit(solution)/shard_map/ppermute | solution.py:19
  71.5 6.2 %collective-permute-start.15 = (bf16[1,2,24,1536]{3,2,1,0:T(8,128)(2,1)S(1)}, bf16[1,2,24,1536]{3,2,1,0:T(8,128)(2,1)S(1)}, u32[]{:S(2)}, u32[]{:S(2)}) collective-permute-start(bf16[1,2,24,1536]{3,2,1,0:T(8,128)(2,1)S(1)} %collective-permute-done.13), channel_id=1, source_target_pairs={{0,15},{1,0},{2,1},{3,2},{4,3},{5,4},{6,5},{7,6},{8,7},{9,8},{10,9... | collective-permute-start | bytes 442376 | tf_op jit(solution)/shard_map/ppermute | solution.py:19
  77.8 4.3 %collective-permute-done.14 = bf16[1,2,24,1536]{3,2,1,0:T(8,128)(2,1)S(1)} collective-permute-done((bf16[1,2,24,1536]{3,2,1,0:T(8,128)(2,1)S(1)}, bf16[1,2,24,1536]{3,2,1,0:T(8,128)(2,1)S(1)}, u32[]{:S(2)}, u32[]{:S(2)}) %collective-permute-start.14) | collective-permute-done | bytes 147488 | tf_op jit(solution)/shard_map/ppermute | solution.py:16
  82.1 9.9 %collective-permute-done.16 = bf16[1,2,24,1536]{3,2,1,0:T(8,128)(2,1)S(1)} collective-permute-done((bf16[1,2,24,1536]{3,2,1,0:T(8,128)(2,1)S(1)}, bf16[1,2,24,1536]{3,2,1,0:T(8,128)(2,1)S(1)}, u32[]{:S(2)}, u32[]{:S(2)}) %collective-permute-start.16) | collective-permute-done | bytes 147488 | tf_op jit(solution)/shard_map/ppermute | solution.py:16
  94.6 11.3 %conditional.4 = (bf16[4,32,384]{2,1,0:T(8,128)(2,1)S(1)}, bf16[128,1536]{1,0:T(8,128)(2,1)S(1)}, bf16[128,384]{1,0:T(8,128)(2,1)S(1)}) conditional(s32[]{:T(128)} %convert_element_type.123, () %tuple.42, (f32[10,38,384]{2,1,0:T(8,128)}, f32[49,384]{1,0:T(8,128)S(1)}, bf16[4,32,384]{2,1,0:T(8,128)(2,1)S(1)}, s32[]{:T(128)}, ...), branch_computations={%region_0.1_spmd, %region_1.6_spmd} | conditional | flops 488964224 | bytes 9118794 | solution.py:198
  94.7 3.3 fusion.113
  105.9 4.4 %collective-permute-start.17 = (bf16[3,32,384]{2,1,0:T(8,128)(2,1)S(1)}, bf16[3,32,384]{2,1,0:T(8,128)(2,1)S(1)}, u32[]{:S(2)}, u32[]{:S(2)}) collective-permute-start(bf16[3,32,384]{2,1,0:T(8,128)(2,1)S(1)} %get-tuple-element.144), channel_id=1, source_target_pairs={{0,1},{1,2},{2,3},{3,4},{4,5},{5,6},{6,7},{7,8},{8,9},{9,10},{10,1... | collective-permute-start | bytes 221192 | tf_op jit(solution)/shard_map/ppermute | solution.py:34
  112.5 4.0 %collective-permute-done.18 = bf16[3,32,384]{2,1,0:T(8,128)(2,1)S(1)} collective-permute-done((bf16[3,32,384]{2,1,0:T(8,128)(2,1)S(1)}, bf16[3,32,384]{2,1,0:T(8,128)(2,1)S(1)}, u32[]{:S(2)}, u32[]{:S(2)}) %collective-permute-start.18) | collective-permute-done | bytes 73760 | tf_op jit(solution)/shard_map/ppermute | solution.py:36
  116.6 6.8 %conditional.5 = (bf16[4,32,384]{2,1,0:T(8,128)(2,1)S(1)}, f32[49,384]{1,0:T(8,128)S(1)}) conditional(s32[]{:T(128)} %convert_element_type.123, () %tuple.41, (bf16[4,32,384]{2,1,0:T(8,128)(2,1)S(1)}, bf16[10,32,384]{2,1,0:T(8,128)(2,1)S(1)}, f32[49,384]{1,0:T(8,128)}, f32[10,38,384]{2,1,0:T(8,128)}, bf16[4,32,384]{2,1,0:T(8,128)(2,1)S(1)}) %tuple.81), branch_computations={%region_6.7_spmd, %region_7.8_spmd} | conditional | flops 57950208 | bytes 4887596 | solution.py:213
  127.9 12.0 %conditional.6 = (bf16[4,32,384]{2,1,0:T(8,128)(2,1)S(1)}, bf16[128,1536]{1,0:T(8,128)(2,1)S(1)}, bf16[128,384]{1,0:T(8,128)(2,1)S(1)}) conditional(s32[]{:T(128)} %convert_element_type.123, () %tuple.45, (f32[10,38,384]{2,1,0:T(8,128)}, f32[49,384]{1,0:T(8,128)S(1)}, bf16[4,32,384]{2,1,0:T(8,128)(2,1)S(1)}, s32[]{:T(128)}, f32[1,2,384]{2,1,0:T(2,128)}, ...), branch_computations={%region_8.9_spmd, %region_9.14_spmd} | conditional | flops 488964224 | bytes 9917570 | solution.py:198
  128.0 3.3 fusion.116
  140.0 4.0 %collective-permute-start.21 = (bf16[3,32,384]{2,1,0:T(8,128)(2,1)S(1)}, bf16[3,32,384]{2,1,0:T(8,128)(2,1)S(1)}, u32[]{:S(2)}, u32[]{:S(2)}) collective-permute-start(bf16[3,32,384]{2,1,0:T(8,128)(2,1)S(1)} %get-tuple-element.142), channel_id=1, source_target_pairs={{0,1},{1,2},{2,3},{3,4},{4,5},{5,6},{6,7},{7,8},{8,9},{9,10},{10,1... | collective-permute-start | bytes 221192 | tf_op jit(solution)/shard_map/ppermute | solution.py:34
  146.5 3.8 collective-permute-done.22
  150.3 4.3 %conditional.7 = (bf16[4,32,384]{2,1,0:T(8,128)(2,1)S(1)}, f32[49,384]{1,0:T(8,128)S(1)}) conditional(s32[]{:T(128)} %convert_element_type.123, () %tuple.40, (bf16[4,32,384]{2,1,0:T(8,128)(2,1)S(1)}, bf16[10,32,384]{2,1,0:T(8,128)(2,1)S(1)}, f32[49,384]{1,0:T(8,128)S(1)}, f32[10,38,384]{2,1,0:T(8,128)S(1)}, ...), branch_computations={%region_14.15_spmd, %region_15.16_spmd} | conditional | flops 57950208 | bytes 2552848 | solution.py:213
  159.5 100.2 %all-reduce.6.cloned.1.call-done = f32[49,384]{1,0:T(8,128)} async-done(((f32[49,384]{1,0:T(8,128)}), f32[49,384]{1,0:T(8,128)}) %all-reduce.6.cloned.1.call-update) | async-done | bytes 75280 | tf_op jit(solution)/shard_map/psum | solution.py:244
  261.3 131.4 %reduce-scatter.2.cloned.1.call-done = f32[96,384]{1,0:T(8,128)} async-done(((f32[1536,384]{1,0:T(8,128)}), f32[96,384]{1,0:T(8,128)}) %reduce-scatter.2.cloned.1.call-update) | async-done | bytes 147472 | tf_op jit(solution)/shard_map/reduce_scatter | solution.py:235
  (171 shorter events, 71.6 us)
Async XLA Ops:
  7.2 87.4 %all-gather.2.cloned.1.call-start = ((), (), s32[]{:S(2)}) async-start(), calls=%async_computation.1 | async-start | bytes 2506752 | tf_op jit(solution)/shard_map/all_gather | solution.py:148
  7.3 13.4 %collective-permute-start.2 = (bf16[1,2,24,1536]{3,2,1,0:T(8,128)(2,1)}, bf16[1,2,24,1536]{3,2,1,0:T(8,128)(2,1)}, u32[]{:S(2)}, u32[]{:S(2)}) collective-permute-start(bf16[1,2,24,1536]{3,2,1,0:T(8,128)(2,1)} %param.26), channel_id=1, source_target_pairs={{0,1},{1,2},{2,3},{3,4},{4,5},{5,6},{6,7},{7,8},{8,9},{9,10},{10,1... | collective-permute-start | bytes 442376 | tf_op jit(solution)/shard_map/ppermute | solution.py:16
  10.2 13.1 %collective-permute-start.3 = (bf16[1,2,24,1536]{3,2,1,0:T(8,128)(2,1)}, bf16[1,2,24,1536]{3,2,1,0:T(8,128)(2,1)S(1)}, u32[]{:S(2)}, u32[]{:S(2)}) collective-permute-start(bf16[1,2,24,1536]{3,2,1,0:T(8,128)(2,1)} %param.26), channel_id=1, source_target_pairs={{0,15},{1,0},{2,1},{3,2},{4,3},{5,4},{6,5},{7,6},{8,7},{9,8},{10,9... | collective-permute-start | bytes 442376 | tf_op jit(solution)/shard_map/ppermute | solution.py:19
  16.9 9.8 %collective-permute-start = (bf16[2,3,32,384]{3,2,1,0:T(8,128)(2,1)}, bf16[2,3,32,384]{3,2,1,0:T(8,128)(2,1)S(1)}, u32[]{:S(2)}, u32[]{:S(2)}) collective-permute-start(bf16[2,3,32,384]{3,2,1,0:T(8,128)(2,1)} %get-tuple-element.140), channel_id=1, source_target_pairs={{0,1},{1,2},{2,3},{3,4},{4,5},{5,6},{6,7},{7,8},{8,9},{9,10},{10,1... | collective-permute-start | bytes 442376 | tf_op jit(solution)/shard_map/ppermute | solution.py:34
  18.2 8.5 %collective-permute-start.1 = (bf16[2,3,32,384]{3,2,1,0:T(8,128)(2,1)}, bf16[2,3,32,384]{3,2,1,0:T(8,128)(2,1)}, u32[]{:S(2)}, u32[]{:S(2)}) collective-permute-start(bf16[2,3,32,384]{3,2,1,0:T(8,128)(2,1)} %get-tuple-element.141), channel_id=1, source_target_pairs={{1,0},{2,1},{3,2},{4,3},{5,4},{6,5},{7,6},{8,7},{9,8},{10,9},{11,1... | collective-permute-start | bytes 442376 | tf_op jit(solution)/shard_map/ppermute | solution.py:36
  19.5 240.3 %all-reduce.6.cloned.1.call-start = ((), (), s32[]{:S(2)}) async-start(), calls=%async_computation.3 | async-start | bytes 172032 | tf_op jit(solution)/shard_map/psum | solution.py:244
  20.6 12.8 %collective-permute-start.4 = (bf16[1,2,24,1536]{3,2,1,0:T(8,128)(2,1)}, bf16[1,2,24,1536]{3,2,1,0:T(8,128)(2,1)S(1)}, u32[]{:S(2)}, u32[]{:S(2)}) collective-permute-start(bf16[1,2,24,1536]{3,2,1,0:T(8,128)(2,1)} %collective-permute-done.2), channel_id=1, source_target_pairs={{0,1},{1,2},{2,3},{3,4},{4,5},{5,6},{6,7},{7,8},{8,9},{9,10},{10,1... | collective-permute-start | bytes 442376 | tf_op jit(solution)/shard_map/ppermute | solution.py:16
  23.3 12.5 %collective-permute-start.5 = (bf16[1,2,24,1536]{3,2,1,0:T(8,128)(2,1)S(1)}, bf16[1,2,24,1536]{3,2,1,0:T(8,128)(2,1)S(1)}, u32[]{:S(2)}, u32[]{:S(2)}) collective-permute-start(bf16[1,2,24,1536]{3,2,1,0:T(8,128)(2,1)S(1)} %collective-permute-done.3), channel_id=1, source_target_pairs={{0,15},{1,0},{2,1},{3,2},{4,3},{5,4},{6,5},{7,6},{8,7},{9,8},{10,9... | collective-permute-start | bytes 442376 | tf_op jit(solution)/shard_map/ppermute | solution.py:19
  33.4 9.5 %collective-permute-start.6 = (bf16[1,2,24,1536]{3,2,1,0:T(8,128)(2,1)S(1)}, bf16[1,2,24,1536]{3,2,1,0:T(8,128)(2,1)S(1)}, u32[]{:S(2)}, u32[]{:S(2)}) collective-permute-start(bf16[1,2,24,1536]{3,2,1,0:T(8,128)(2,1)S(1)} %collective-permute-done.4), channel_id=1, source_target_pairs={{0,1},{1,2},{2,3},{3,4},{4,5},{5,6},{6,7},{7,8},{8,9},{9,10},{10,1... | collective-permute-start | bytes 442376 | tf_op jit(solution)/shard_map/ppermute | solution.py:16
  35.8 8.5 %collective-permute-start.7 = (bf16[1,2,24,1536]{3,2,1,0:T(8,128)(2,1)S(1)}, bf16[1,2,24,1536]{3,2,1,0:T(8,128)(2,1)S(1)}, u32[]{:S(2)}, u32[]{:S(2)}) collective-permute-start(bf16[1,2,24,1536]{3,2,1,0:T(8,128)(2,1)S(1)} %collective-permute-done.5), channel_id=1, source_target_pairs={{0,15},{1,0},{2,1},{3,2},{4,3},{5,4},{6,5},{7,6},{8,7},{9,8},{10,9... | collective-permute-start | bytes 442376 | tf_op jit(solution)/shard_map/ppermute | solution.py:19
  43.0 8.9 %collective-permute-start.8 = (bf16[1,2,24,1536]{3,2,1,0:T(8,128)(2,1)S(1)}, bf16[1,2,24,1536]{3,2,1,0:T(8,128)(2,1)S(1)}, u32[]{:S(2)}, u32[]{:S(2)}) collective-permute-start(bf16[1,2,24,1536]{3,2,1,0:T(8,128)(2,1)S(1)} %collective-permute-done.6), channel_id=1, source_target_pairs={{0,1},{1,2},{2,3},{3,4},{4,5},{5,6},{6,7},{7,8},{8,9},{9,10},{10,1... | collective-permute-start | bytes 442376 | tf_op jit(solution)/shard_map/ppermute | solution.py:16
  44.3 7.8 %collective-permute-start.9 = (bf16[1,2,24,1536]{3,2,1,0:T(8,128)(2,1)S(1)}, bf16[1,2,24,1536]{3,2,1,0:T(8,128)(2,1)S(1)}, u32[]{:S(2)}, u32[]{:S(2)}) collective-permute-start(bf16[1,2,24,1536]{3,2,1,0:T(8,128)(2,1)S(1)} %collective-permute-done.7), channel_id=1, source_target_pairs={{0,15},{1,0},{2,1},{3,2},{4,3},{5,4},{6,5},{7,6},{8,7},{9,8},{10,9... | collective-permute-start | bytes 442376 | tf_op jit(solution)/shard_map/ppermute | solution.py:19
  51.9 9.4 %collective-permute-start.10 = (bf16[1,2,24,1536]{3,2,1,0:T(8,128)(2,1)S(1)}, bf16[1,2,24,1536]{3,2,1,0:T(8,128)(2,1)S(1)}, u32[]{:S(2)}, u32[]{:S(2)}) collective-permute-start(bf16[1,2,24,1536]{3,2,1,0:T(8,128)(2,1)S(1)} %collective-permute-done.8), channel_id=1, source_target_pairs={{0,1},{1,2},{2,3},{3,4},{4,5},{5,6},{6,7},{7,8},{8,9},{9,10},{10,1... | collective-permute-start | bytes 442376 | tf_op jit(solution)/shard_map/ppermute | solution.py:16
  52.1 10.7 %collective-permute-start.11 = (bf16[1,2,24,1536]{3,2,1,0:T(8,128)(2,1)S(1)}, bf16[1,2,24,1536]{3,2,1,0:T(8,128)(2,1)S(1)}, u32[]{:S(2)}, u32[]{:S(2)}) collective-permute-start(bf16[1,2,24,1536]{3,2,1,0:T(8,128)(2,1)S(1)} %collective-permute-done.9), channel_id=1, source_target_pairs={{0,15},{1,0},{2,1},{3,2},{4,3},{5,4},{6,5},{7,6},{8,7},{9,8},{10,9... | collective-permute-start | bytes 442376 | tf_op jit(solution)/shard_map/ppermute | solution.py:19
  61.3 8.8 %collective-permute-start.12 = (bf16[1,2,24,1536]{3,2,1,0:T(8,128)(2,1)S(1)}, bf16[1,2,24,1536]{3,2,1,0:T(8,128)(2,1)S(1)}, u32[]{:S(2)}, u32[]{:S(2)}) collective-permute-start(bf16[1,2,24,1536]{3,2,1,0:T(8,128)(2,1)S(1)} %collective-permute-done.10), channel_id=1, source_target_pairs={{0,1},{1,2},{2,3},{3,4},{4,5},{5,6},{6,7},{7,8},{8,9},{9,10},{10,1... | collective-permute-start | bytes 442376 | tf_op jit(solution)/shard_map/ppermute | solution.py:16
  62.8 8.7 %collective-permute-start.13 = (bf16[1,2,24,1536]{3,2,1,0:T(8,128)(2,1)S(1)}, bf16[1,2,24,1536]{3,2,1,0:T(8,128)(2,1)S(1)}, u32[]{:S(2)}, u32[]{:S(2)}) collective-permute-start(bf16[1,2,24,1536]{3,2,1,0:T(8,128)(2,1)S(1)} %collective-permute-done.11), channel_id=1, source_target_pairs={{0,15},{1,0},{2,1},{3,2},{4,3},{5,4},{6,5},{7,6},{8,7},{9,8},{10,9... | collective-permute-start | bytes 442376 | tf_op jit(solution)/shard_map/ppermute | solution.py:19
  70.1 11.9 %collective-permute-start.14 = (bf16[1,2,24,1536]{3,2,1,0:T(8,128)(2,1)S(1)}, bf16[1,2,24,1536]{3,2,1,0:T(8,128)(2,1)S(1)}, u32[]{:S(2)}, u32[]{:S(2)}) collective-permute-start(bf16[1,2,24,1536]{3,2,1,0:T(8,128)(2,1)S(1)} %collective-permute-done.12), channel_id=1, source_target_pairs={{0,1},{1,2},{2,3},{3,4},{4,5},{5,6},{6,7},{7,8},{8,9},{9,10},{10,1... | collective-permute-start | bytes 442376 | tf_op jit(solution)/shard_map/ppermute | solution.py:16
  71.5 10.5 %collective-permute-start.15 = (bf16[1,2,24,1536]{3,2,1,0:T(8,128)(2,1)S(1)}, bf16[1,2,24,1536]{3,2,1,0:T(8,128)(2,1)S(1)}, u32[]{:S(2)}, u32[]{:S(2)}) collective-permute-start(bf16[1,2,24,1536]{3,2,1,0:T(8,128)(2,1)S(1)} %collective-permute-done.13), channel_id=1, source_target_pairs={{0,15},{1,0},{2,1},{3,2},{4,3},{5,4},{6,5},{7,6},{8,7},{9,8},{10,9... | collective-permute-start | bytes 442376 | tf_op jit(solution)/shard_map/ppermute | solution.py:19
  82.0 9.9 %collective-permute-start.16 = (bf16[1,2,24,1536]{3,2,1,0:T(8,128)(2,1)S(1)}, bf16[1,2,24,1536]{3,2,1,0:T(8,128)(2,1)S(1)}, u32[]{:S(2)}, u32[]{:S(2)}) collective-permute-start(bf16[1,2,24,1536]{3,2,1,0:T(8,128)(2,1)S(1)} %collective-permute-done.14), channel_id=1, source_target_pairs={{0,1},{1,2},{2,3},{3,4},{4,5},{5,6},{6,7},{7,8},{8,9},{9,10},{10,1... | collective-permute-start | bytes 442376 | tf_op jit(solution)/shard_map/ppermute | solution.py:16
  105.9 6.6 %collective-permute-start.17 = (bf16[3,32,384]{2,1,0:T(8,128)(2,1)S(1)}, bf16[3,32,384]{2,1,0:T(8,128)(2,1)S(1)}, u32[]{:S(2)}, u32[]{:S(2)}) collective-permute-start(bf16[3,32,384]{2,1,0:T(8,128)(2,1)S(1)} %get-tuple-element.144), channel_id=1, source_target_pairs={{0,1},{1,2},{2,3},{3,4},{4,5},{5,6},{6,7},{7,8},{8,9},{9,10},{10,1... | collective-permute-start | bytes 221192 | tf_op jit(solution)/shard_map/ppermute | solution.py:34
  110.3 6.2 %collective-permute-start.18 = (bf16[3,32,384]{2,1,0:T(8,128)(2,1)S(1)}, bf16[3,32,384]{2,1,0:T(8,128)(2,1)S(1)}, u32[]{:S(2)}, u32[]{:S(2)}) collective-permute-start(bf16[3,32,384]{2,1,0:T(8,128)(2,1)S(1)} %get-tuple-element.145), channel_id=1, source_target_pairs={{1,0},{2,1},{3,2},{4,3},{5,4},{6,5},{7,6},{8,7},{9,8},{10,9},{11,1... | collective-permute-start | bytes 221192 | tf_op jit(solution)/shard_map/ppermute | solution.py:36
  140.0 6.5 %collective-permute-start.21 = (bf16[3,32,384]{2,1,0:T(8,128)(2,1)S(1)}, bf16[3,32,384]{2,1,0:T(8,128)(2,1)S(1)}, u32[]{:S(2)}, u32[]{:S(2)}) collective-permute-start(bf16[3,32,384]{2,1,0:T(8,128)(2,1)S(1)} %get-tuple-element.142), channel_id=1, source_target_pairs={{0,1},{1,2},{2,3},{3,4},{4,5},{5,6},{6,7},{7,8},{8,9},{9,10},{10,1... | collective-permute-start | bytes 221192 | tf_op jit(solution)/shard_map/ppermute | solution.py:34
  146.4 10.3 %collective-permute-start.23 = (bf16[128,1920]{1,0:T(8,128)(2,1)S(1)}, bf16[128,1920]{1,0:T(8,128)(2,1)S(1)}, u32[]{:S(2)}, u32[]{:S(2)}) collective-permute-start(bf16[128,1920]{1,0:T(8,128)(2,1)S(1)} %pad_maximum_fusion.1), channel_id=1, source_target_pairs={{0,16},{16,0},{1,17},{17,1},{2,18},{18,2},{3,19},{19,3},{4,20},{20... | collective-permute-start | bytes 1474568 | tf_op jit(solution)/shard_map/ppermute | solution.py:60
  156.6 236.2 %reduce-scatter.2.cloned.1.call-start = ((), (), s32[]{:S(2)}) async-start(), calls=%async_computation.2 | async-start | bytes 2506752 | tf_op jit(solution)/shard_map/reduce_scatter | solution.py:235
  (22 other events, 444.7 us)
Sparse Core Ops, SparseCore 0:
  19.6 74.9 all-gather.1
  156.7 102.9 all-reduce.5
  265.2 127.4 reduce-scatter.1
